TPU v7x, 32 devices: a whole 2x2x4 slice. The times are simulated.
32 devices in a mesh: tile: 8 (over z, y), spec: 4 (over x, core).
Axes of the slice: x: 2, y: 2, z: 4, core: 2. Of those that a mesh axis runs over, the one named last changes fastest.
Arguments:
- grad_columns: bfloat16 [8192, 512], P('tile', 'spec'), may hold values from -6 to 6
- grad_flux: float32 [16, 8192], P('spec', 'tile'), may hold values from -6 to 6
- remap_part: int32 [8192, 4], P('tile'), may hold values from 0 to 7, all different within a row; in each aligned block of 1024 rows (0 to 1023, 1024 to 2047, ...) at most 1024 rows name the same one
- remap_slot: int32 [8192, 4], P('tile'), may hold values from 0 to 1023
- remap_weight: float32 [8192, 4], P('tile'), may hold values from 0.2 to 1
- col_count: int32 [8], P('tile'), may hold values from 341 to 1024, as said below
- neighbors: int32 [8192, 4], P('tile'), may hold values from 0 to 1279, as said below
- kappa: float32 [16], P('spec'), may hold values from 0.03 to 0.2
- thickness: float32 [16, 32], P('spec'), may hold values from 0.2 to 2
- vertical: bfloat16 [16, 32, 32], P('spec'), may hold values from -1 to 1
- reaction: bfloat16 [16, 16], P(None, 'spec'), may hold values from -1.5 to 1.5
Outputs:
- grad_state: bfloat16 [8192, 512], P('tile', 'spec')
- grad_bottom: float32 [16, 8192], P('spec', 'tile')
Inputs may be any that keep to these rules, and one draw needn't show every extreme that they name: `remap_part`: each coarse cell names 4 different partitions; the entries of the cells of one tile (1024 cells) name one partition at most 1024 times. `col_count`: live counts of partitions differ up to threefold; one partition holds 1024 live columns and one holds 341. `neighbors`: row p * 1024 + i lists the codes of 4 neighbours of slot i of partition p; every named slot is live; the first partition names no previous and the last no next partition.
All inputs are finite; a program needn't handle non-finite values.
Results may differ from a plain program's by a relative error of at most 0.008.
Values may be sent and summed in bfloat16 or wider, within the bound.
No kernel may reach another device: no remote copies, remote signals or barrier semaphores. Data moves between devices by JAX's collectives and lax.ppermute only.
A program may use at most 128 MiB of HBM per device.

v0:
```python
import functools

import jax
import jax.numpy as jnp
from jax import lax
from jax.experimental import pallas as pl
from jax.experimental.pallas import tpu as pltpu
from jax.sharding import PartitionSpec as P

SUB = 4
LANES = 128
WIDE = 256
OWN = 16
DEAD = 15
F32 = jnp.float32
BF16 = jnp.bfloat16
VMEM = pl.BlockSpec(memory_space=pltpu.VMEM)
HBM = pl.BlockSpec(memory_space=pltpu.HBM)
SMEM = pl.BlockSpec(memory_space=pltpu.SMEM)
LIMIT = 40 * 1024 * 1024
MOST = 60 * 1024 * 1024


def call(kernel, outs, specs, scratch=(), flops=0, moved=0, limit=LIMIT):
    return pl.pallas_call(
        kernel,
        out_shape=outs,
        in_specs=specs,
        out_specs=[VMEM] * len(outs),
        scratch_shapes=scratch,
        compiler_params=pltpu.CompilerParams(vmem_limit_bytes=limit),
        cost_estimate=pl.CostEstimate(flops=flops, bytes_accessed=moved, transcendentals=0),
    )


def nt(a, b, precision=None):
    return lax.dot_general(
        a, b, (((1,), (1,)), ((), ())), precision=precision, preferred_element_type=F32
    )


def nn(a, b, precision=None):
    return lax.dot_general(
        a, b, (((1,), (0,)), ((), ())), precision=precision, preferred_element_type=F32
    )


def row_ids(rows, cols):
    return lax.broadcasted_iota(jnp.int32, (rows, cols), 0)


def fetch(pairs, sems):
    copies = [pltpu.make_async_copy(a, b, sems.at[i]) for i, (a, b) in enumerate(pairs)]
    for copy in copies:
        copy.start()
    for copy in copies:
        copy.wait()


def coded(ints):
    value = (128 + (ints & 127)).astype(F32)
    for bit in range(4):
        value = value * jnp.where((ints >> (7 + bit)) & 1 == 1, float(2 ** (2**bit)), 1.0)
    return value


def decoded(value):
    high = jnp.zeros(value.shape, jnp.int32)
    for bit in (8, 4, 2, 1):
        large = value >= 128.0 * 2.0**bit
        value = jnp.where(large, value * 2.0**-bit, value)
        high = high + jnp.where(large, bit, 0)
    return value - 128.0, high


def hot(key, ids):
    return jnp.where(ids == key, jnp.ones((), BF16), jnp.zeros((), BF16))


def picked(keys, value, target):
    return jnp.where(keys == jnp.asarray(target, BF16), value, jnp.zeros((), BF16))


def narrow(ints):
    return ints.astype(F32).astype(BF16)


def folded(rows):
    middle = rows.shape[1] // 2
    return [rows[:, :middle], rows[:, middle:]]


def prepare(
    count_ref, kappa_ref, gc_any, vert_any, thick_any, flux_any, part_any, slot_any, weight_any,
    nbr_any, reaction_any, payload_ref, misc_ref, remap_ref,
    gc_ref, vert_ref, thick_ref, flux_ref, part_ref, slot_ref, weight_ref, nbr_ref, reaction_ref,
    sems,
):
    fetch(
        [
            (gc_any, gc_ref),
            (vert_any, vert_ref),
            (thick_any, thick_ref),
            (flux_any, flux_ref),
            (part_any, part_ref),
            (slot_any, slot_ref),
            (weight_any, weight_ref),
            (nbr_any, nbr_ref),
            (reaction_any, reaction_ref),
        ],
        sems,
    )
    tiles = payload_ref.shape[0]
    col_max = gc_ref.shape[0]
    species, layers, _ = vert_ref.shape
    width = species * layers
    subs = col_max // WIDE

    v = vert_ref[...].astype(F32).reshape(width, layers)
    v = jnp.concatenate([v] * species, axis=1)
    rows = row_ids(width, width) // layers
    cols = lax.broadcasted_iota(jnp.int32, (width, width), 1) // layers
    vt = jnp.where(rows == cols, v, 0.0).T.astype(BF16)
    hi = lax.Precision.HIGHEST
    v2 = nn(vt, vt)
    v4 = nn(v2, v2, hi)
    th = jnp.concatenate([thick_ref[s : s + 1, :] for s in range(species)], axis=1)
    misc_ref[0:8] = nt(jnp.broadcast_to(th, (8, width)), v4, hi)
    rates = [jnp.full((1, width), kappa_ref[s], F32) for s in range(species)]
    mix = reaction_ref[...].astype(F32)
    mix = jnp.concatenate([mix, jnp.zeros((4, width - mix.shape[1]), F32)], axis=1)
    misc_ref[8:16] = jnp.concatenate(rates + [mix], axis=0)
    live = lax.broadcasted_iota(jnp.int32, (1, col_max), 1) < count_ref[0]
    w = jnp.where(live, nt(v4.astype(BF16), gc_ref[...]), 0.0)

    flux, weight = flux_ref[...], weight_ref[...]
    slot = slot_ref[...]
    part, sub, low = part_ref[...], slot // WIDE, slot % WIDE
    remap_ref[...] = jnp.concatenate(
        [low.astype(F32), part.astype(F32), sub.astype(F32), weight], axis=0
    )
    low = narrow(low)
    ids = narrow(row_ids(WIDE, 1))
    place = row_ids(16, 1)
    sums = jnp.zeros((species * subs * tiles, WIDE), F32)
    for r in range(4):
        value = flux * weight[r : r + 1]
        value = [jnp.broadcast_to(value[s : s + 1], (16, col_max)).astype(BF16) for s in range(4)]
        spot = sub[r : r + 1] * tiles + part[r : r + 1]
        keys = [narrow(spot - place - 16 * k) for k in range(subs * tiles // 16)]
        blocks = [picked(key, value[s], 0) for s in range(species) for key in keys]
        sums = sums + nt(jnp.concatenate(blocks, axis=0), hot(low[r : r + 1], ids))

    nbr = jnp.where(live, nbr_ref[...], DEAD * LANES)
    tail = folded(coded(nbr))
    for q in range(tiles):
        s = q * OWN // layers
        mine = sums[s * subs * tiles : (s + 1) * subs * tiles]
        mine = jnp.concatenate([mine[h * tiles : (h + 1) * tiles] for h in range(subs)], axis=1)
        pieces = folded(w[q * OWN : (q + 1) * OWN]) + folded(mine) + tail
        payload_ref[q] = jnp.concatenate(pieces, axis=0).astype(BF16)


def unfolded(block, first, rows):
    return jnp.concatenate([block[first : first + rows], block[first + rows : first + 2 * rows]], axis=1)


def chain(tiles, layers, misc_ref, data_ref, back_ref, x_ref, hot_ref, high_ref):
    col_max = x_ref.shape[3]
    blocks = col_max // LANES
    me = lax.axis_index("tile")
    ids = narrow(row_ids(LANES, 1))

    lane = lax.broadcasted_iota(jnp.int32, (OWN, misc_ref.shape[1]), 1)
    row = row_ids(OWN, 1)
    tv_own = jnp.where(lane == me * OWN + row, misc_ref[0:1], 0.0)
    tv_own = jnp.sum(tv_own, axis=1, keepdims=True)
    mine = me * OWN // layers
    rate = jnp.zeros((1, 1), F32)
    for s in range(4):
        rate = jnp.where(mine == s, misc_ref[8 + s : 9 + s, 0:1], rate)

    inj = jnp.zeros((tiles, col_max), F32)
    for q in range(tiles):
        block = data_ref[q].astype(F32)
        inj = inj + unfolded(block, 2 * OWN, tiles)
    for q in range(tiles):
        block = data_ref[q].astype(F32)
        low, high = decoded(unfolded(block, 2 * OWN + 2 * tiles, 4))
        live = high[0:1] != DEAD
        x_ref[0, q] = unfolded(block, 0, OWN) + tv_own * jnp.where(live, inj[q : q + 1], 0.0)
        high_ref[q] = high.astype(F32)
        for n in range(4):
            hot_ref[q * 4 + n] = hot(low[n : n + 1].astype(BF16), ids)

    for step in range(SUB):
        here, there = step % 2, (step + 1) % 2
        for q in range(tiles):
            x_ref[there, q] = (1.0 - 4.0 * rate) * x_ref[here, q]
        for q in range(tiles):
            high = high_ref[q]
            value = (rate * x_ref[here, q]).astype(BF16)
            total = jnp.zeros(((blocks + 2) * OWN, LANES), F32)
            for n in range(4):
                key = jnp.broadcast_to(high[n : n + 1], (OWN, col_max)).astype(BF16)
                rows = [picked(key, value, h) for h in range(blocks + 2)]
                total = total + nt(jnp.concatenate(rows, axis=0), hot_ref[q * 4 + n])
            mine_rows = [total[h * OWN : (h + 1) * OWN] for h in range(blocks)]
            x_ref[there, q] += jnp.concatenate(mine_rows, axis=1)
            if q > 0:
                cross = total[blocks * OWN : (blocks + 1) * OWN]
                x_ref[there, q - 1, :, LANES : 2 * LANES] += cross
            if q < tiles - 1:
                x_ref[there, q + 1, :, :LANES] += total[(blocks + 1) * OWN :]
    last = SUB % 2
    quarters = col_max // WIDE
    mix = jnp.concatenate([misc_ref[8:16], misc_ref[8:16]], axis=1)[4:8]
    mix = jnp.concatenate([mix, mix], axis=0)
    for g in range(quarters):
        top = [
            x_ref[last, tiles // quarters * g + h, 0:1, k * WIDE : (k + 1) * WIDE]
            for h in range(tiles // quarters)
            for k in range(quarters)
        ]
        top = jnp.where((me * OWN) % layers == 0, jnp.concatenate(top, axis=0), mix)
        for q in range(tiles):
            piece = x_ref[last, q, :, g * WIDE : (g + 1) * WIDE]
            back_ref[q * quarters + g] = jnp.concatenate([piece, top], axis=0).astype(BF16)


def middle(tiles, parts, layers, data_ref, remap_ref, out_ref):
    col_max = remap_ref.shape[1]
    quarters = col_max // WIDE
    halves = layers // OWN
    species = 4 * parts
    me = lax.axis_index("spec")

    def source(s, half):
        return ((s % 4) * halves + half) * parts + s // 4

    mix = [data_ref[source(4 * k, 1), OWN:].astype(F32)[0:4, 0:species] for k in range(parts)]
    mix = jnp.concatenate(mix, axis=0)
    size = species * OWN
    left = row_ids(size, species) // OWN == lax.broadcasted_iota(jnp.int32, (size, species), 1)
    right = row_ids(species, size) == lax.broadcasted_iota(jnp.int32, (species, size), 1) // OWN
    left, right = (jnp.where(hit, 1.0, 0.0).astype(BF16) for hit in (left, right))
    full = nn(nn(left, mix.astype(BF16)).astype(BF16), right)
    same = row_ids(size, size) % OWN == lax.broadcasted_iota(jnp.int32, (size, size), 1) % OWN
    full = jnp.where(same, full, 0.0).astype(BF16)
    mixed = []
    for half in range(halves):
        x = [data_ref[source(s, half), 0:OWN] for s in range(species)]
        mixed.append(nn(full, jnp.concatenate(x, axis=0)))

    table = [data_ref[source(s, 0), OWN:].astype(F32) for s in range(species)]
    table = jnp.concatenate(table, axis=0).astype(BF16)
    low = remap_ref[0:4].astype(BF16)
    place = remap_ref[4:8].astype(jnp.int32) * quarters + remap_ref[8:12].astype(jnp.int32)
    place = place - me * tiles
    ids = narrow(row_ids(WIDE, 1))
    totals = [jnp.zeros((tiles, col_max), F32) for s in range(species)]
    for r in range(4):
        found = nn(table, hot(low[r : r + 1], ids))
        weight = jnp.where(
            place[r : r + 1] == row_ids(tiles, 1), remap_ref[12 + r : 13 + r], 0.0
        )
        for s in range(species):
            totals[s] = totals[s] + found[s * tiles : (s + 1) * tiles] * weight
    bottom = [jnp.sum(total, axis=0, keepdims=True) for total in totals]
    bottom = nn(mix, jnp.concatenate(bottom, axis=0), lax.Precision.HIGHEST)
    for k in range(parts):
        rows = []
        for t in range(4 * k, 4 * k + 4):
            rows += [mixed[half][t * OWN : (t + 1) * OWN] for half in range(halves)]
        mine = bottom[4 * k : 4 * k + 4]
        rows += [mine[:, h * WIDE : (h + 1) * WIDE] for h in range(quarters)]
        out_ref[k] = jnp.concatenate(rows, axis=0).astype(BF16)


def settle(all_ref, state_ref, bottom_ref):
    parts, rows, wide = all_ref.shape
    width = state_ref.shape[1]
    total = jnp.zeros((rows - width, wide), F32)
    for k in range(parts):
        state = all_ref[k, 0:width].astype(F32)
        state_ref[k * wide : (k + 1) * wide, :] = state.T.astype(BF16)
        total = total + all_ref[k, width:].astype(F32)
    pieces = [total[h * 4 : h * 4 + 4] for h in range(parts)]
    bottom_ref[...] = jnp.concatenate(pieces, axis=1)


def shifted(block, axis, distance):
    devices = range(lax.axis_size(axis))
    route = [(i - distance, i) for i in devices if i - distance in devices]
    return lax.ppermute(block, axis, route)


def halo_body(
    grad_columns,
    grad_flux,
    remap_part,
    remap_slot,
    remap_weight,
    col_count,
    neighbors,
    kappa,
    thickness,
    vertical,
    reaction,
):
    tiles = lax.axis_size("tile")
    col_max = grad_columns.shape[0]
    rim_width = col_max // 8
    species = kappa.shape[0]
    layers = thickness.shape[1]
    width = species * layers
    cells, per_cell = remap_part.shape
    entries = cells * per_cell
    capacity = 2 * entries // tiles
    nbr_count = neighbors.shape[1]
    dest_flat = remap_part.reshape(-1)
    slot_flat = remap_slot.reshape(-1)
    dest_table = (dest_flat[:, None] == jnp.arange(tiles, dtype=jnp.int32)[None, :]).astype(
        jnp.int32
    )
    earlier = jnp.cumsum(dest_table, axis=0) - dest_table
    rank_within = jnp.sum(earlier * dest_table, axis=1)
    bucket_pos = dest_flat * capacity + rank_within
    entry_values = (remap_weight[:, :, None] * grad_flux.T[:, None, :]).reshape(entries, species)
    send_values = (
        jnp.zeros((tiles * capacity, species), jnp.float32)
        .at[bucket_pos]
        .set(entry_values)
        .reshape(tiles, capacity, species)
    )
    send_slots = (
        jnp.full((tiles * capacity, 1), col_max, jnp.int32)
        .at[bucket_pos]
        .set(slot_flat[:, None])
        .reshape(tiles, capacity, 1)
    )
    recv_values, recv_slots = (
        lax.all_to_all(send_values, "tile", split_axis=0, concat_axis=0, tiled=True),
        lax.all_to_all(send_slots, "tile", split_axis=0, concat_axis=0, tiled=True),
    )
    slot_index = recv_slots.reshape(-1)
    injected = (
        jnp.zeros((col_max + 1, species), jnp.float32)
        .at[slot_index]
        .add(recv_values.reshape(-1, species))[:col_max]
    )
    live_mask = (jnp.arange(col_max) < col_count[0]).astype(jnp.float32)[:, None]
    adjoint = live_mask * (
        grad_columns.astype(jnp.float32)
        + (injected[:, :, None] * thickness[None, :, :]).reshape(col_max, width)
    )
    rate_row = jnp.repeat(kappa, layers)[None, :]
    eye_block = jnp.eye(species, dtype=jnp.bfloat16)
    block_operator = jnp.einsum("slm,st->sltm", vertical, eye_block).reshape(width, width)
    target_rows = jnp.arange(col_max + 2 * rim_width, dtype=jnp.int32)[:, None]
    count_matrix = jnp.zeros((col_max + 2 * rim_width, col_max), jnp.float32)
    for column in range(nbr_count):
        count_matrix = count_matrix + (neighbors[:, column][None, :] == target_rows).astype(
            jnp.float32
        )
    zero_rest = jnp.zeros((col_max - 2 * rim_width, width), jnp.float32)
    for substep in range(SUB):
        spread = rate_row * adjoint
        extended = jnp.dot(
            count_matrix,
            spread,
            precision=lax.Precision.HIGHEST,
            preferred_element_type=jnp.float32,
        )
        to_previous = extended[col_max : col_max + rim_width]
        to_following = extended[col_max + rim_width :]
        from_following = shifted(to_previous.astype(jnp.bfloat16), "tile", -1).astype(
            to_previous.dtype
        )
        from_previous = shifted(to_following.astype(jnp.bfloat16), "tile", 1).astype(
            to_following.dtype
        )
        rim_terms = jnp.concatenate([from_previous, from_following, zero_rest], axis=0)
        bedload = adjoint - nbr_count * rate_row * adjoint + extended[:col_max] + rim_terms
        adjoint = jnp.dot(
            bedload.astype(jnp.bfloat16), block_operator, preferred_element_type=jnp.float32
        )
    rounded = adjoint.astype(jnp.bfloat16)
    piece = lax.all_gather(rounded, "spec", axis=1, tiled=True)
    piece_species = piece.shape[1] // layers
    mixed = jnp.einsum(
        "jsl,st->jtl",
        piece.reshape(col_max, piece_species, layers),
        reaction,
        preferred_element_type=jnp.float32,
    )
    grad_state = mixed.reshape(col_max, width).astype(jnp.bfloat16)
    top_layer = mixed[:, :, 0]
    everything = lax.all_gather(top_layer, "tile", axis=0, tiled=True)
    picked = everything[dest_flat * col_max + slot_flat]
    grad_bottom = jnp.sum(
        picked.reshape(cells, per_cell, species) * remap_weight[:, :, None], axis=1
    ).T
    return (grad_state, grad_bottom)


def column_body(
    grad_columns,
    grad_flux,
    remap_part,
    remap_slot,
    remap_weight,
    col_count,
    neighbors,
    kappa,
    thickness,
    vertical,
    reaction,
):
    tiles = lax.axis_size("tile")
    parts = lax.axis_size("spec")
    col_max, width = grad_columns.shape
    layers = thickness.shape[1]
    shape = jax.ShapeDtypeStruct
    moved = [grad_columns, vertical, thickness, grad_flux]
    moved += [remap_part.T, remap_slot.T, remap_weight.T, neighbors.T, reaction.T]
    payload, misc, remap = call(
        prepare,
        [
            shape((tiles, 2 * (OWN + tiles + 4), col_max // 2), BF16),
            shape((16, width), F32),
            shape((16, col_max), F32),
        ],
        [SMEM] * 2 + [HBM] * 9,
        scratch=[pltpu.VMEM(a.shape, a.dtype) for a in moved] + [pltpu.SemaphoreType.DMA((9,))],
        flops=4 * 10**7,
        moved=10**6,
        limit=MOST,
    )(col_count, kappa, *moved)
    data = lax.all_to_all(payload, "tile", split_axis=0, concat_axis=0, tiled=True)
    back = call(
        functools.partial(chain, tiles, layers),
        [shape((tiles * parts, OWN + tiles, WIDE), BF16)],
        [VMEM] * 2,
        scratch=[
            pltpu.VMEM((2, tiles, OWN, col_max), F32),
            pltpu.VMEM((tiles * 4, LANES, col_max), BF16),
            pltpu.VMEM((tiles, 4, col_max), F32),
        ],
        flops=10**10,
        moved=10**6,
    )(misc, data)[0]
    home = lax.all_to_all(back, ("tile", "spec"), split_axis=0, concat_axis=0, tiled=True)
    packed = call(
        functools.partial(middle, tiles, parts, layers),
        [shape((parts, width + OWN, WIDE), BF16)],
        [VMEM] * 2,
        flops=10**9,
        moved=10**6,
    )(home, remap)[0]
    every = lax.all_to_all(packed, "spec", split_axis=0, concat_axis=0, tiled=True)
    outs = [shape((col_max, width), BF16), shape((4, col_max), F32)]
    return tuple(call(settle, outs, [VMEM], flops=10**8, moved=10**6)(every))


def body(*args):
    tiles, parts = lax.axis_size("tile"), lax.axis_size("spec")
    layers = args[8].shape[1]
    fits = tiles == 8 and layers == 2 * OWN and args[0].shape == (parts * WIDE, tiles * OWN)
    return (column_body if fits else halo_body)(*args)


def solution(mesh):
    placed = (
        P("tile", "spec"),
        P("spec", "tile"),
        P("tile", None),
        P("tile", None),
        P("tile", None),
        P("tile"),
        P("tile", None),
        P("spec"),
        P("spec", None),
        P("spec", None, None),
        P(None, "spec"),
    )
    return jax.shard_map(
        body,
        mesh=mesh,
        in_specs=placed,
        out_specs=(P("tile", "spec"), P("spec", "tile")),
        check_vma=False,
    )
```

profile of v0, /device:TPU:0, one launch (start us, length us, event | category | flops | bytes accessed | tf_op | source)
XLA Modules:
  0.0 65.5 jit_solution(12043167223835930270)
XLA Ops:
  1.3 3.9 %shard_map.122 = (bf16[8,56,512]{2,1,0:T(8,128)(2,1)}, f32[16,128]{1,0:T(8,128)}, f32[16,1024]{1,0:T(8,128)}) custom-call(s32[1]{0:T(128)S(6)} %copy.13.count_ref, f32[4]{0:T(128)} %kappa_ref.1, bf16[1024,128]{1,0:T(8,128)(2,1)} %gc_any.1, bf16[4,32,32]{2,1,0:T(8,128)(2,1)} %vert_any.1, f32[4,32]{1,0:T(4,128)} %thick_any.1, f32[4,1024]{1,0:T(4,128)} %flux_any.1, ...), custom_call_target="tpu_custom_call" | custom-call | flops 40000000 | bytes 1000000 | tf_op jit(solution)/shard_map/pallas_call | solution.py:427
  5.2 0.0 copy-start.1
  5.2 20.5 %all_to_all.15.data_ref = bf16[8,56,512]{2,1,0:T(8,128)(2,1)S(1)} all-to-all(bf16[8,56,512]{2,1,0:T(8,128)(2,1)} %get-tuple-element.6), channel_id=1, replica_groups=mesh['tile'=8,'spec'=4] {'tile'}, dimensions={0} | all-to-all | bytes 917504 | tf_op jit(solution)/shard_map/all_to_all | solution.py:440
  25.7 0.0 copy-done.1
  25.7 12.7 %shard_map.123 = bf16[32,24,256]{2,1,0:T(8,128)(2,1)S(1)} custom-call(f32[16,128]{1,0:T(8,128)S(1)} %copy-done.1, bf16[8,56,512]{2,1,0:T(8,128)(2,1)S(1)} %all_to_all.15.data_ref), custom_call_target="tpu_custom_call" | custom-call | flops 10000000000 | bytes 1000000 | tf_op jit(solution)/shard_map/pallas_call | solution.py:441
  38.4 0.0 copy-start
  38.4 16.5 %all_to_all.16.data_ref = bf16[32,24,256]{2,1,0:T(8,128)(2,1)S(1)} all-to-all(bf16[32,24,256]{2,1,0:T(8,128)(2,1)S(1)} %shard_map.123), channel_id=1, replica_groups=mesh['tile'=8,'spec'=4] {'tile','spec'}, dimensions={0} | all-to-all | bytes 786432 | tf_op jit(solution)/shard_map/all_to_all | solution.py:453
  54.9 0.0 copy-done
  54.9 1.0 %shard_map.124 = bf16[4,144,256]{2,1,0:T(8,128)(2,1)S(1)} custom-call(bf16[32,24,256]{2,1,0:T(8,128)(2,1)S(1)} %all_to_all.16.data_ref, f32[16,1024]{1,0:T(8,128)S(1)} %copy-done), custom_call_target="tpu_custom_call" | custom-call | flops 1000000000 | bytes 1000000 | tf_op jit(solution)/shard_map/pallas_call | solution.py:454
  55.9 8.8 %all_to_all.17.all_ref = bf16[4,144,256]{2,1,0:T(8,128)(2,1)S(1)} all-to-all(bf16[4,144,256]{2,1,0:T(8,128)(2,1)S(1)} %shard_map.124), channel_id=1, replica_groups=mesh['tile'=8,'spec'=4] {'spec'}, dimensions={0} | all-to-all | bytes 589824 | tf_op jit(solution)/shard_map/all_to_all | solution.py:461
  64.6 0.8 %shard_map.125 = (bf16[1024,128]{1,0:T(8,128)(2,1)}, f32[4,1024]{1,0:T(4,128)}) custom-call(bf16[4,144,256]{2,1,0:T(8,128)(2,1)S(1)} %all_to_all.17.all_ref), custom_call_target="tpu_custom_call" | custom-call | flops 100000000 | bytes 1000000 | tf_op jit(solution)/shard_map/pallas_call | solution.py:463
Async XLA Ops:
  5.2 20.5 %copy-start.1 = (f32[16,128]{1,0:T(8,128)S(1)}, f32[16,128]{1,0:T(8,128)}, u32[]{:S(2)}) copy-start(f32[16,128]{1,0:T(8,128)} %get-tuple-element.5.misc_ref) | copy-start | bytes 24580
  38.4 16.5 %copy-start = (f32[16,1024]{1,0:T(8,128)S(1)}, f32[16,1024]{1,0:T(8,128)}, u32[]{:S(2)}) copy-start(f32[16,1024]{1,0:T(8,128)} %get-tuple-element.7.remap_ref) | copy-start | bytes 196612
where the time goes:
time: 65.8 us; the launch traced here: 65.5 us
  blocking collectives  45.8 us (70%)
  Pallas kernels  18.4 us (28%)
  between operations  1.31 us (2%)
    all_to_all x1, blocking collectives, column_body(): lax.all_to_all(payload, 'tile', split_axis=0, concat_axis=0, tiled=True)  20.5 us
    all_to_all x1, blocking collectives, column_body(): lax.all_to_all(back, ('tile', 'spec'), split_axis=0, concat_axis=0, tiled...  16.5 us
    pallas_call x1, Pallas kernels, column_body(): call(functools.partial(chain, tiles, layers), [shape((tiles * parts, OWN...  12.7 us
    all_to_all x1, blocking collectives, column_body(): lax.all_to_all(packed, 'spec', split_axis=0, concat_axis=0, tiled=True)  8.76 us
    pallas_call x1, Pallas kernels, column_body(): call(prepare, [shape((tiles, 2 * (OWN + tiles + 4), col_max // 2), BF16),...  3.9 us

commit v1 on v0

--- a/solution.py
+++ b/solution.py
@@ -21,12 +21,12 @@
 MOST = 60 * 1024 * 1024
 
 
-def call(kernel, outs, specs, scratch=(), flops=0, moved=0, limit=LIMIT):
+def call(kernel, outs, specs, scratch=(), flops=0, moved=0, limit=LIMIT, first=VMEM):
     return pl.pallas_call(
         kernel,
         out_shape=outs,
         in_specs=specs,
-        out_specs=[VMEM] * len(outs),
+        out_specs=[first] + [VMEM] * (len(outs) - 1),
         scratch_shapes=scratch,
         compiler_params=pltpu.CompilerParams(vmem_limit_bytes=limit),
         cost_estimate=pl.CostEstimate(flops=flops, bytes_accessed=moved, transcendentals=0),
@@ -49,12 +49,11 @@
     return lax.broadcasted_iota(jnp.int32, (rows, cols), 0)
 
 
-def fetch(pairs, sems):
+def started(pairs, sems):
     copies = [pltpu.make_async_copy(a, b, sems.at[i]) for i, (a, b) in enumerate(pairs)]
     for copy in copies:
         copy.start()
-    for copy in copies:
-        copy.wait()
+    return copies
 
 
 def coded(ints):
@@ -92,24 +91,26 @@
 
 def prepare(
     count_ref, kappa_ref, gc_any, vert_any, thick_any, flux_any, part_any, slot_any, weight_any,
-    nbr_any, reaction_any, payload_ref, misc_ref, remap_ref,
+    nbr_any, reaction_any, payload_any, misc_ref, remap_ref,
     gc_ref, vert_ref, thick_ref, flux_ref, part_ref, slot_ref, weight_ref, nbr_ref, reaction_ref,
-    sems,
+    payload_ref, sems, out_sems,
 ):
-    fetch(
+    copies = started(
         [
-            (gc_any, gc_ref),
             (vert_any, vert_ref),
             (thick_any, thick_ref),
+            (reaction_any, reaction_ref),
+            (slot_any, slot_ref),
+            (part_any, part_ref),
+            (weight_any, weight_ref),
             (flux_any, flux_ref),
-            (part_any, part_ref),
-            (slot_any, slot_ref),
-            (weight_any, weight_ref),
             (nbr_any, nbr_ref),
-            (reaction_any, reaction_ref),
+            (gc_any, gc_ref),
         ],
         sems,
     )
+    for copy in copies[:-1]:
+        copy.wait()
     tiles = payload_ref.shape[0]
     col_max = gc_ref.shape[0]
     species, layers, _ = vert_ref.shape
@@ -130,9 +131,6 @@
     mix = reaction_ref[...].astype(F32)
     mix = jnp.concatenate([mix, jnp.zeros((4, width - mix.shape[1]), F32)], axis=1)
     misc_ref[8:16] = jnp.concatenate(rates + [mix], axis=0)
-    live = lax.broadcasted_iota(jnp.int32, (1, col_max), 1) < count_ref[0]
-    w = jnp.where(live, nt(v4.astype(BF16), gc_ref[...]), 0.0)
-
     flux, weight = flux_ref[...], weight_ref[...]
     slot = slot_ref[...]
     part, sub, low = part_ref[...], slot // WIDE, slot % WIDE
@@ -151,14 +149,21 @@
         blocks = [picked(key, value[s], 0) for s in range(species) for key in keys]
         sums = sums + nt(jnp.concatenate(blocks, axis=0), hot(low[r : r + 1], ids))
 
-    nbr = jnp.where(live, nbr_ref[...], DEAD * LANES)
-    tail = folded(coded(nbr))
+    live = lax.broadcasted_iota(jnp.int32, (1, col_max), 1) < count_ref[0]
+    tail = folded(coded(jnp.where(live, nbr_ref[...], DEAD * LANES)))
+    copies[-1].wait()
+    w = jnp.where(live, nt(v4.astype(BF16), gc_ref[...]), 0.0)
+    sent = []
     for q in range(tiles):
         s = q * OWN // layers
         mine = sums[s * subs * tiles : (s + 1) * subs * tiles]
         mine = jnp.concatenate([mine[h * tiles : (h + 1) * tiles] for h in range(subs)], axis=1)
         pieces = folded(w[q * OWN : (q + 1) * OWN]) + folded(mine) + tail
         payload_ref[q] = jnp.concatenate(pieces, axis=0).astype(BF16)
+        sent.append(pltpu.make_async_copy(payload_ref.at[q], payload_any.at[q], out_sems.at[q]))
+        sent[-1].start()
+    for copy in sent:
+        copy.wait()
 
 
 def unfolded(block, first, rows):
@@ -193,25 +198,34 @@
         for n in range(4):
             hot_ref[q * 4 + n] = hot(low[n : n + 1].astype(BF16), ids)
 
+    def product(here, q):
+        high = high_ref[q]
+        value = (rate * x_ref[here, q]).astype(BF16)
+        hits = list(range(blocks)) + [blocks] * (q > 0) + [blocks + 1] * (q < tiles - 1)
+        total = jnp.zeros((len(hits) * OWN, LANES), F32)
+        for n in range(4):
+            key = jnp.broadcast_to(high[n : n + 1], (OWN, col_max)).astype(BF16)
+            rows = [picked(key, value, h) for h in hits]
+            total = total + nt(jnp.concatenate(rows, axis=0), hot_ref[q * 4 + n])
+        pieces = [total[i * OWN : (i + 1) * OWN] for i in range(len(hits))]
+        own = pieces[:blocks]
+        to_prev = pieces[blocks] if q > 0 else None
+        to_next = pieces[-1] if q < tiles - 1 else None
+        return own, to_prev, to_next
+
     for step in range(SUB):
         here, there = step % 2, (step + 1) % 2
+        from_prev = None
+        current = product(here, 0)
         for q in range(tiles):
-            x_ref[there, q] = (1.0 - 4.0 * rate) * x_ref[here, q]
-        for q in range(tiles):
-            high = high_ref[q]
-            value = (rate * x_ref[here, q]).astype(BF16)
-            total = jnp.zeros(((blocks + 2) * OWN, LANES), F32)
-            for n in range(4):
-                key = jnp.broadcast_to(high[n : n + 1], (OWN, col_max)).astype(BF16)
-                rows = [picked(key, value, h) for h in range(blocks + 2)]
-                total = total + nt(jnp.concatenate(rows, axis=0), hot_ref[q * 4 + n])
-            mine_rows = [total[h * OWN : (h + 1) * OWN] for h in range(blocks)]
-            x_ref[there, q] += jnp.concatenate(mine_rows, axis=1)
-            if q > 0:
-                cross = total[blocks * OWN : (blocks + 1) * OWN]
-                x_ref[there, q - 1, :, LANES : 2 * LANES] += cross
-            if q < tiles - 1:
-                x_ref[there, q + 1, :, :LANES] += total[(blocks + 1) * OWN :]
+            following = product(here, q + 1) if q < tiles - 1 else None
+            own, _, to_next = current
+            if from_prev is not None:
+                own[0] = own[0] + from_prev
+            if following is not None:
+                own[1] = own[1] + following[1]
+            x_ref[there, q] = (1.0 - 4.0 * rate) * x_ref[here, q] + jnp.concatenate(own, axis=1)
+            from_prev, current = to_next, following
     last = SUB % 2
     quarters = col_max // WIDE
     mix = jnp.concatenate([misc_ref[8:16], misc_ref[8:16]], axis=1)[4:8]
@@ -238,7 +252,7 @@
     def source(s, half):
         return ((s % 4) * halves + half) * parts + s // 4
 
-    mix = [data_ref[source(4 * k, 1), OWN:].astype(F32)[0:4, 0:species] for k in range(parts)]
+    mix = [data_ref[source(4 * k, 1)].astype(F32)[OWN : OWN + 4, 0:species] for k in range(parts)]
     mix = jnp.concatenate(mix, axis=0)
     size = species * OWN
     left = row_ids(size, species) // OWN == lax.broadcasted_iota(jnp.int32, (size, species), 1)
@@ -252,7 +266,7 @@
         x = [data_ref[source(s, half), 0:OWN] for s in range(species)]
         mixed.append(nn(full, jnp.concatenate(x, axis=0)))
 
-    table = [data_ref[source(s, 0), OWN:].astype(F32) for s in range(species)]
+    table = [data_ref[source(s, 0)].astype(F32)[OWN:] for s in range(species)]
     table = jnp.concatenate(table, axis=0).astype(BF16)
     low = remap_ref[0:4].astype(BF16)
     place = remap_ref[4:8].astype(jnp.int32) * quarters + remap_ref[8:12].astype(jnp.int32)
@@ -432,10 +446,13 @@
             shape((16, col_max), F32),
         ],
         [SMEM] * 2 + [HBM] * 9,
-        scratch=[pltpu.VMEM(a.shape, a.dtype) for a in moved] + [pltpu.SemaphoreType.DMA((9,))],
+        scratch=[pltpu.VMEM(a.shape, a.dtype) for a in moved]
+        + [pltpu.VMEM((tiles, 2 * (OWN + tiles + 4), col_max // 2), BF16)]
+        + [pltpu.SemaphoreType.DMA((9,)), pltpu.SemaphoreType.DMA((tiles,))],
         flops=4 * 10**7,
         moved=10**6,
         limit=MOST,
+        first=HBM,
     )(col_count, kappa, *moved)
     data = lax.all_to_all(payload, "tile", split_axis=0, concat_axis=0, tiled=True)
     back = call(

time: 65.8 us -> 64.8 us (0.985)
  Pallas kernels: 18.4 us -> 17.3 us
    pallas_call x1, Pallas kernels: 12.7 us -> 10.9 us  [column_body(): call(functools.partial(chain, tiles, layers), [shape((tiles * parts, OWN...]
    pallas_call x1, Pallas kernels: 3.9 us -> 4.59 us  [column_body(): call(prepare, [shape((tiles, 2 * (OWN + tiles + 4), col_max // 2), BF16),...]
where the time goes in v1:
time: 64.8 us; the launch traced here: 64.4 us
  blocking collectives  45.8 us (71%)
  Pallas kernels  17.3 us (27%)
  between operations  1.31 us (2%)
    all_to_all x1, blocking collectives, column_body(): lax.all_to_all(payload, 'tile', split_axis=0, concat_axis=0, tiled=True)  20.5 us
    all_to_all x1, blocking collectives, column_body(): lax.all_to_all(back, ('tile', 'spec'), split_axis=0, concat_axis=0, tiled...  16.5 us
    pallas_call x1, Pallas kernels, column_body(): call(functools.partial(chain, tiles, layers), [shape((tiles * parts, OWN...  10.9 us
    all_to_all x1, blocking collectives, column_body(): lax.all_to_all(packed, 'spec', split_axis=0, concat_axis=0, tiled=True)  8.76 us
    pallas_call x1, Pallas kernels, column_body(): call(prepare, [shape((tiles, 2 * (OWN + tiles + 4), col_max // 2), BF16),...  4.59 us

profile of v1, /device:TPU:0, one launch (start us, length us, event | category | flops | bytes accessed | tf_op | source)
XLA Modules:
  0.0 64.4 jit_solution(11009070787311503762)
XLA Ops:
  1.3 4.6 %shard_map.122 = (bf16[8,56,512]{2,1,0:T(8,128)(2,1)}, f32[16,128]{1,0:T(8,128)}, f32[16,1024]{1,0:T(8,128)}) custom-call(s32[1]{0:T(128)S(6)} %copy.13.count_ref, f32[4]{0:T(128)} %kappa_ref.1, bf16[1024,128]{1,0:T(8,128)(2,1)} %gc_any.1, bf16[4,32,32]{2,1,0:T(8,128)(2,1)} %vert_any.1, f32[4,32]{1,0:T(4,128)} %thick_any.1, f32[4,1024]{1,0:T(4,128)} %flux_any.1, ...), custom_call_target="tpu_custom_call" | custom-call | flops 40000000 | bytes 1000000 | tf_op jit(solution)/shard_map/pallas_call | solution.py:441
  5.9 0.0 copy-start.1
  5.9 20.5 %all_to_all.15.data_ref = bf16[8,56,512]{2,1,0:T(8,128)(2,1)S(1)} all-to-all(bf16[8,56,512]{2,1,0:T(8,128)(2,1)} %get-tuple-element.6), channel_id=1, replica_groups=mesh['tile'=8,'spec'=4] {'tile'}, dimensions={0} | all-to-all | bytes 917504 | tf_op jit(solution)/shard_map/all_to_all | solution.py:457
  26.4 0.0 copy-done.1
  26.4 10.9 %shard_map.123 = bf16[32,24,256]{2,1,0:T(8,128)(2,1)S(1)} custom-call(f32[16,128]{1,0:T(8,128)S(1)} %copy-done.1, bf16[8,56,512]{2,1,0:T(8,128)(2,1)S(1)} %all_to_all.15.data_ref), custom_call_target="tpu_custom_call" | custom-call | flops 10000000000 | bytes 1000000 | tf_op jit(solution)/shard_map/pallas_call | solution.py:458
  37.3 0.0 copy-start
  37.3 16.5 %all_to_all.16.data_ref = bf16[32,24,256]{2,1,0:T(8,128)(2,1)S(1)} all-to-all(bf16[32,24,256]{2,1,0:T(8,128)(2,1)S(1)} %shard_map.123), channel_id=1, replica_groups=mesh['tile'=8,'spec'=4] {'tile','spec'}, dimensions={0} | all-to-all | bytes 786432 | tf_op jit(solution)/shard_map/all_to_all | solution.py:470
  53.8 0.0 copy-done
  53.8 1.0 %shard_map.124 = bf16[4,144,256]{2,1,0:T(8,128)(2,1)S(1)} custom-call(bf16[32,24,256]{2,1,0:T(8,128)(2,1)S(1)} %all_to_all.16.data_ref, f32[16,1024]{1,0:T(8,128)S(1)} %copy-done), custom_call_target="tpu_custom_call" | custom-call | flops 1000000000 | bytes 1000000 | tf_op jit(solution)/shard_map/pallas_call | solution.py:471
  54.8 8.8 %all_to_all.17.all_ref = bf16[4,144,256]{2,1,0:T(8,128)(2,1)S(1)} all-to-all(bf16[4,144,256]{2,1,0:T(8,128)(2,1)S(1)} %shard_map.124), channel_id=1, replica_groups=mesh['tile'=8,'spec'=4] {'spec'}, dimensions={0} | all-to-all | bytes 589824 | tf_op jit(solution)/shard_map/all_to_all | solution.py:478
  63.6 0.8 %shard_map.125 = (bf16[1024,128]{1,0:T(8,128)(2,1)}, f32[4,1024]{1,0:T(4,128)}) custom-call(bf16[4,144,256]{2,1,0:T(8,128)(2,1)S(1)} %all_to_all.17.all_ref), custom_call_target="tpu_custom_call" | custom-call | flops 100000000 | bytes 1000000 | tf_op jit(solution)/shard_map/pallas_call | solution.py:480
Async XLA Ops:
  5.9 20.5 %copy-start.1 = (f32[16,128]{1,0:T(8,128)S(1)}, f32[16,128]{1,0:T(8,128)}, u32[]{:S(2)}) copy-start(f32[16,128]{1,0:T(8,128)} %get-tuple-element.5.misc_ref) | copy-start | bytes 24580
  37.3 16.5 %copy-start = (f32[16,1024]{1,0:T(8,128)S(1)}, f32[16,1024]{1,0:T(8,128)}, u32[]{:S(2)}) copy-start(f32[16,1024]{1,0:T(8,128)} %get-tuple-element.7.remap_ref) | copy-start | bytes 196612

commit v2 on v1

--- a/solution.py
+++ b/solution.py
@@ -21,12 +21,12 @@
 MOST = 60 * 1024 * 1024
 
 
-def call(kernel, outs, specs, scratch=(), flops=0, moved=0, limit=LIMIT, first=VMEM):
+def call(kernel, outs, specs, scratch=(), flops=0, moved=0, limit=LIMIT):
     return pl.pallas_call(
         kernel,
         out_shape=outs,
         in_specs=specs,
-        out_specs=[first] + [VMEM] * (len(outs) - 1),
+        out_specs=[VMEM] * len(outs),
         scratch_shapes=scratch,
         compiler_params=pltpu.CompilerParams(vmem_limit_bytes=limit),
         cost_estimate=pl.CostEstimate(flops=flops, bytes_accessed=moved, transcendentals=0),
@@ -91,9 +91,9 @@
 
 def prepare(
     count_ref, kappa_ref, gc_any, vert_any, thick_any, flux_any, part_any, slot_any, weight_any,
-    nbr_any, reaction_any, payload_any, misc_ref, remap_ref,
+    nbr_any, reaction_any, payload_ref, misc_ref, remap_ref,
     gc_ref, vert_ref, thick_ref, flux_ref, part_ref, slot_ref, weight_ref, nbr_ref, reaction_ref,
-    payload_ref, sems, out_sems,
+    sems,
 ):
     copies = started(
         [
@@ -109,7 +109,7 @@
         ],
         sems,
     )
-    for copy in copies[:-1]:
+    for copy in copies:
         copy.wait()
     tiles = payload_ref.shape[0]
     col_max = gc_ref.shape[0]
@@ -151,19 +151,13 @@
 
     live = lax.broadcasted_iota(jnp.int32, (1, col_max), 1) < count_ref[0]
     tail = folded(coded(jnp.where(live, nbr_ref[...], DEAD * LANES)))
-    copies[-1].wait()
     w = jnp.where(live, nt(v4.astype(BF16), gc_ref[...]), 0.0)
-    sent = []
     for q in range(tiles):
         s = q * OWN // layers
         mine = sums[s * subs * tiles : (s + 1) * subs * tiles]
         mine = jnp.concatenate([mine[h * tiles : (h + 1) * tiles] for h in range(subs)], axis=1)
         pieces = folded(w[q * OWN : (q + 1) * OWN]) + folded(mine) + tail
         payload_ref[q] = jnp.concatenate(pieces, axis=0).astype(BF16)
-        sent.append(pltpu.make_async_copy(payload_ref.at[q], payload_any.at[q], out_sems.at[q]))
-        sent[-1].start()
-    for copy in sent:
-        copy.wait()
 
 
 def unfolded(block, first, rows):
@@ -446,13 +440,10 @@
             shape((16, col_max), F32),
         ],
         [SMEM] * 2 + [HBM] * 9,
-        scratch=[pltpu.VMEM(a.shape, a.dtype) for a in moved]
-        + [pltpu.VMEM((tiles, 2 * (OWN + tiles + 4), col_max // 2), BF16)]
-        + [pltpu.SemaphoreType.DMA((9,)), pltpu.SemaphoreType.DMA((tiles,))],
+        scratch=[pltpu.VMEM(a.shape, a.dtype) for a in moved] + [pltpu.SemaphoreType.DMA((9,))],
         flops=4 * 10**7,
         moved=10**6,
         limit=MOST,
-        first=HBM,
     )(col_count, kappa, *moved)
     data = lax.all_to_all(payload, "tile", split_axis=0, concat_axis=0, tiled=True)
     back = call(

time: 64.8 us -> 64.2 us (level)
  no operation moved by 1% of the time
where the time goes in v2:
time: 64.2 us; the launch traced here: 63.9 us
  blocking collectives  45.8 us (71%)
  Pallas kernels  16.8 us (26%)
  between operations  1.31 us (2%)
    all_to_all x1, blocking collectives, column_body(): lax.all_to_all(payload, 'tile', split_axis=0, concat_axis=0, tiled=True)  20.5 us
    all_to_all x1, blocking collectives, column_body(): lax.all_to_all(back, ('tile', 'spec'), split_axis=0, concat_axis=0, tiled...  16.5 us
    pallas_call x1, Pallas kernels, column_body(): call(functools.partial(chain, tiles, layers), [shape((tiles * parts, OWN...  10.9 us
    all_to_all x1, blocking collectives, column_body(): lax.all_to_all(packed, 'spec', split_axis=0, concat_axis=0, tiled=True)  8.76 us
    pallas_call x1, Pallas kernels, column_body(): call(prepare, [shape((tiles, 2 * (OWN + tiles + 4), col_max // 2), BF16),...  4.02 us

profile of v2, /device:TPU:0, one launch (start us, length us, event | category | flops | bytes accessed | tf_op | source)
XLA Modules:
  0.0 63.9 jit_solution(4940893667899554376)
XLA Ops:
  1.3 4.0 %shard_map.122 = (bf16[8,56,512]{2,1,0:T(8,128)(2,1)}, f32[16,128]{1,0:T(8,128)}, f32[16,1024]{1,0:T(8,128)}) custom-call(s32[1]{0:T(128)S(6)} %copy.13.count_ref, f32[4]{0:T(128)} %kappa_ref.1, bf16[1024,128]{1,0:T(8,128)(2,1)} %gc_any.1, bf16[4,32,32]{2,1,0:T(8,128)(2,1)} %vert_any.1, f32[4,32]{1,0:T(4,128)} %thick_any.1, f32[4,1024]{1,0:T(4,128)} %flux_any.1, ...), custom_call_target="tpu_custom_call" | custom-call | flops 40000000 | bytes 1000000 | tf_op jit(solution)/shard_map/pallas_call | solution.py:435
  5.3 0.0 copy-start.1
  5.3 20.5 %all_to_all.15.data_ref = bf16[8,56,512]{2,1,0:T(8,128)(2,1)S(1)} all-to-all(bf16[8,56,512]{2,1,0:T(8,128)(2,1)} %get-tuple-element.6), channel_id=1, replica_groups=mesh['tile'=8,'spec'=4] {'tile'}, dimensions={0} | all-to-all | bytes 917504 | tf_op jit(solution)/shard_map/all_to_all | solution.py:448
  25.8 0.0 copy-done.1
  25.8 10.9 %shard_map.123 = bf16[32,24,256]{2,1,0:T(8,128)(2,1)S(1)} custom-call(f32[16,128]{1,0:T(8,128)S(1)} %copy-done.1, bf16[8,56,512]{2,1,0:T(8,128)(2,1)S(1)} %all_to_all.15.data_ref), custom_call_target="tpu_custom_call" | custom-call | flops 10000000000 | bytes 1000000 | tf_op jit(solution)/shard_map/pallas_call | solution.py:449
  36.8 0.0 copy-start
  36.8 16.5 %all_to_all.16.data_ref = bf16[32,24,256]{2,1,0:T(8,128)(2,1)S(1)} all-to-all(bf16[32,24,256]{2,1,0:T(8,128)(2,1)S(1)} %shard_map.123), channel_id=1, replica_groups=mesh['tile'=8,'spec'=4] {'tile','spec'}, dimensions={0} | all-to-all | bytes 786432 | tf_op jit(solution)/shard_map/all_to_all | solution.py:461
  53.3 0.0 copy-done
  53.3 1.0 %shard_map.124 = bf16[4,144,256]{2,1,0:T(8,128)(2,1)S(1)} custom-call(bf16[32,24,256]{2,1,0:T(8,128)(2,1)S(1)} %all_to_all.16.data_ref, f32[16,1024]{1,0:T(8,128)S(1)} %copy-done), custom_call_target="tpu_custom_call" | custom-call | flops 1000000000 | bytes 1000000 | tf_op jit(solution)/shard_map/pallas_call | solution.py:462
  54.3 8.8 %all_to_all.17.all_ref = bf16[4,144,256]{2,1,0:T(8,128)(2,1)S(1)} all-to-all(bf16[4,144,256]{2,1,0:T(8,128)(2,1)S(1)} %shard_map.124), channel_id=1, replica_groups=mesh['tile'=8,'spec'=4] {'spec'}, dimensions={0} | all-to-all | bytes 589824 | tf_op jit(solution)/shard_map/all_to_all | solution.py:469
  63.0 0.8 %shard_map.125 = (bf16[1024,128]{1,0:T(8,128)(2,1)}, f32[4,1024]{1,0:T(4,128)}) custom-call(bf16[4,144,256]{2,1,0:T(8,128)(2,1)S(1)} %all_to_all.17.all_ref), custom_call_target="tpu_custom_call" | custom-call | flops 100000000 | bytes 1000000 | tf_op jit(solution)/shard_map/pallas_call | solution.py:471
Async XLA Ops:
  5.3 20.5 %copy-start.1 = (f32[16,128]{1,0:T(8,128)S(1)}, f32[16,128]{1,0:T(8,128)}, u32[]{:S(2)}) copy-start(f32[16,128]{1,0:T(8,128)} %get-tuple-element.5.misc_ref) | copy-start | bytes 24580
  36.8 16.5 %copy-start = (f32[16,1024]{1,0:T(8,128)S(1)}, f32[16,1024]{1,0:T(8,128)}, u32[]{:S(2)}) copy-start(f32[16,1024]{1,0:T(8,128)} %get-tuple-element.7.remap_ref) | copy-start | bytes 196612

commit v3 on v2

--- a/solution.py
+++ b/solution.py
@@ -164,7 +164,7 @@
     return jnp.concatenate([block[first : first + rows], block[first + rows : first + 2 * rows]], axis=1)
 
 
-def chain(tiles, layers, misc_ref, data_ref, back_ref, x_ref, hot_ref, high_ref):
+def chain(tiles, layers, misc_ref, data_ref, back_ref, x_ref, hot_ref, key_ref):
     col_max = x_ref.shape[3]
     blocks = col_max // LANES
     me = lax.axis_index("tile")
@@ -183,24 +183,26 @@
     for q in range(tiles):
         block = data_ref[q].astype(F32)
         inj = inj + unfolded(block, 2 * OWN, tiles)
-    for q in range(tiles):
+
+    def start(q):
         block = data_ref[q].astype(F32)
         low, high = decoded(unfolded(block, 2 * OWN + 2 * tiles, 4))
         live = high[0:1] != DEAD
         x_ref[0, q] = unfolded(block, 0, OWN) + tv_own * jnp.where(live, inj[q : q + 1], 0.0)
-        high_ref[q] = high.astype(F32)
+        high = high.astype(F32)
         for n in range(4):
-            hot_ref[q * 4 + n] = hot(low[n : n + 1].astype(BF16), ids)
-
-    def product(here, q):
-        high = high_ref[q]
-        value = (rate * x_ref[here, q]).astype(BF16)
+            cols = slice(n * col_max, (n + 1) * col_max)
+            key_ref[q, :, cols] = jnp.broadcast_to(high[n : n + 1], (OWN, col_max)).astype(BF16)
+            hot_ref[q, :, cols] = hot(low[n : n + 1].astype(BF16), ids)
+
+    def product(step, q):
+        if step == 0:
+            start(q)
+        value = (rate * x_ref[step % 2, q]).astype(BF16)
+        value = jnp.concatenate([value] * 4, axis=1)
         hits = list(range(blocks)) + [blocks] * (q > 0) + [blocks + 1] * (q < tiles - 1)
-        total = jnp.zeros((len(hits) * OWN, LANES), F32)
-        for n in range(4):
-            key = jnp.broadcast_to(high[n : n + 1], (OWN, col_max)).astype(BF16)
-            rows = [picked(key, value, h) for h in hits]
-            total = total + nt(jnp.concatenate(rows, axis=0), hot_ref[q * 4 + n])
+        rows = [picked(key_ref[q], value, h) for h in hits]
+        total = nt(jnp.concatenate(rows, axis=0), hot_ref[q])
         pieces = [total[i * OWN : (i + 1) * OWN] for i in range(len(hits))]
         own = pieces[:blocks]
         to_prev = pieces[blocks] if q > 0 else None
@@ -210,9 +212,9 @@
     for step in range(SUB):
         here, there = step % 2, (step + 1) % 2
         from_prev = None
-        current = product(here, 0)
+        current = product(step, 0)
         for q in range(tiles):
-            following = product(here, q + 1) if q < tiles - 1 else None
+            following = product(step, q + 1) if q < tiles - 1 else None
             own, _, to_next = current
             if from_prev is not None:
                 own[0] = own[0] + from_prev
@@ -452,8 +454,8 @@
         [VMEM] * 2,
         scratch=[
             pltpu.VMEM((2, tiles, OWN, col_max), F32),
-            pltpu.VMEM((tiles * 4, LANES, col_max), BF16),
-            pltpu.VMEM((tiles, 4, col_max), F32),
+            pltpu.VMEM((tiles, LANES, 4 * col_max), BF16),
+            pltpu.VMEM((tiles, OWN, 4 * col_max), BF16),
         ],
         flops=10**10,
         moved=10**6,

time: 64.2 us -> 64.3 us (level)
  no operation moved by 1% of the time
where the time goes in v3:
time: 64.3 us; the launch traced here: 63.9 us
  blocking collectives  45.8 us (71%)
  Pallas kernels  16.8 us (26%)
  between operations  1.31 us (2%)
    all_to_all x1, blocking collectives, column_body(): lax.all_to_all(payload, 'tile', split_axis=0, concat_axis=0, tiled=True)  20.5 us
    all_to_all x1, blocking collectives, column_body(): lax.all_to_all(back, ('tile', 'spec'), split_axis=0, concat_axis=0, tiled...  16.5 us
    pallas_call x1, Pallas kernels, column_body(): call(functools.partial(chain, tiles, layers), [shape((tiles * parts, OWN...  11 us
    all_to_all x1, blocking collectives, column_body(): lax.all_to_all(packed, 'spec', split_axis=0, concat_axis=0, tiled=True)  8.76 us
    pallas_call x1, Pallas kernels, column_body(): call(prepare, [shape((tiles, 2 * (OWN + tiles + 4), col_max // 2), BF16),...  4.02 us

profile of v3, /device:TPU:0, one launch (start us, length us, event | category | flops | bytes accessed | tf_op | source)
XLA Modules:
  0.0 63.9 jit_solution(9431981133502589577)
XLA Ops:
  1.3 4.0 %shard_map.122 = (bf16[8,56,512]{2,1,0:T(8,128)(2,1)}, f32[16,128]{1,0:T(8,128)}, f32[16,1024]{1,0:T(8,128)}) custom-call(s32[1]{0:T(128)S(6)} %copy.13.count_ref, f32[4]{0:T(128)} %kappa_ref.1, bf16[1024,128]{1,0:T(8,128)(2,1)} %gc_any.1, bf16[4,32,32]{2,1,0:T(8,128)(2,1)} %vert_any.1, f32[4,32]{1,0:T(4,128)} %thick_any.1, f32[4,1024]{1,0:T(4,128)} %flux_any.1, ...), custom_call_target="tpu_custom_call" | custom-call | flops 40000000 | bytes 1000000 | tf_op jit(solution)/shard_map/pallas_call | solution.py:437
  5.3 0.0 copy-start.1
  5.3 20.5 %all_to_all.15.data_ref = bf16[8,56,512]{2,1,0:T(8,128)(2,1)S(1)} all-to-all(bf16[8,56,512]{2,1,0:T(8,128)(2,1)} %get-tuple-element.6), channel_id=1, replica_groups=mesh['tile'=8,'spec'=4] {'tile'}, dimensions={0} | all-to-all | bytes 917504 | tf_op jit(solution)/shard_map/all_to_all | solution.py:450
  25.8 0.0 copy-done.1
  25.8 11.0 %shard_map.123 = bf16[32,24,256]{2,1,0:T(8,128)(2,1)S(1)} custom-call(f32[16,128]{1,0:T(8,128)S(1)} %copy-done.1, bf16[8,56,512]{2,1,0:T(8,128)(2,1)S(1)} %all_to_all.15.data_ref), custom_call_target="tpu_custom_call" | custom-call | flops 10000000000 | bytes 1000000 | tf_op jit(solution)/shard_map/pallas_call | solution.py:451
  36.8 0.0 copy-start
  36.8 16.5 %all_to_all.16.data_ref = bf16[32,24,256]{2,1,0:T(8,128)(2,1)S(1)} all-to-all(bf16[32,24,256]{2,1,0:T(8,128)(2,1)S(1)} %shard_map.123), channel_id=1, replica_groups=mesh['tile'=8,'spec'=4] {'tile','spec'}, dimensions={0} | all-to-all | bytes 786432 | tf_op jit(solution)/shard_map/all_to_all | solution.py:463
  53.3 0.0 copy-done
  53.3 1.0 %shard_map.124 = bf16[4,144,256]{2,1,0:T(8,128)(2,1)S(1)} custom-call(bf16[32,24,256]{2,1,0:T(8,128)(2,1)S(1)} %all_to_all.16.data_ref, f32[16,1024]{1,0:T(8,128)S(1)} %copy-done), custom_call_target="tpu_custom_call" | custom-call | flops 1000000000 | bytes 1000000 | tf_op jit(solution)/shard_map/pallas_call | solution.py:464
  54.3 8.8 %all_to_all.17.all_ref = bf16[4,144,256]{2,1,0:T(8,128)(2,1)S(1)} all-to-all(bf16[4,144,256]{2,1,0:T(8,128)(2,1)S(1)} %shard_map.124), channel_id=1, replica_groups=mesh['tile'=8,'spec'=4] {'spec'}, dimensions={0} | all-to-all | bytes 589824 | tf_op jit(solution)/shard_map/all_to_all | solution.py:471
  63.1 0.8 %shard_map.125 = (bf16[1024,128]{1,0:T(8,128)(2,1)}, f32[4,1024]{1,0:T(4,128)}) custom-call(bf16[4,144,256]{2,1,0:T(8,128)(2,1)S(1)} %all_to_all.17.all_ref), custom_call_target="tpu_custom_call" | custom-call | flops 100000000 | bytes 1000000 | tf_op jit(solution)/shard_map/pallas_call | solution.py:473
Async XLA Ops:
  5.3 20.5 %copy-start.1 = (f32[16,128]{1,0:T(8,128)S(1)}, f32[16,128]{1,0:T(8,128)}, u32[]{:S(2)}) copy-start(f32[16,128]{1,0:T(8,128)} %get-tuple-element.5.misc_ref) | copy-start | bytes 24580
  36.8 16.5 %copy-start = (f32[16,1024]{1,0:T(8,128)S(1)}, f32[16,1024]{1,0:T(8,128)}, u32[]{:S(2)}) copy-start(f32[16,1024]{1,0:T(8,128)} %get-tuple-element.7.remap_ref) | copy-start | bytes 196612

commit v4 on v2

--- a/solution.py
+++ b/solution.py
@@ -90,13 +90,15 @@
 
 
 def prepare(
-    count_ref, kappa_ref, gc_any, vert_any, thick_any, flux_any, part_any, slot_any, weight_any,
+    count_ref, kappa_any, gc_any, vert_any, thick_any, flux_any, part_any, slot_any, weight_any,
     nbr_any, reaction_any, payload_ref, misc_ref, remap_ref,
-    gc_ref, vert_ref, thick_ref, flux_ref, part_ref, slot_ref, weight_ref, nbr_ref, reaction_ref,
-    sems,
+    kappa_ref, gc_ref, vert_ref, thick_ref, flux_ref, part_ref, slot_ref, weight_ref,
+    nbr_ref, reaction_ref, sems,
 ):
     copies = started(
         [
+            (gc_any, gc_ref),
+            (kappa_any, kappa_ref),
             (vert_any, vert_ref),
             (thick_any, thick_ref),
             (reaction_any, reaction_ref),
@@ -105,7 +107,6 @@
             (weight_any, weight_ref),
             (flux_any, flux_ref),
             (nbr_any, nbr_ref),
-            (gc_any, gc_ref),
         ],
         sems,
     )
@@ -439,8 +440,10 @@
             shape((16, width), F32),
             shape((16, col_max), F32),
         ],
-        [SMEM] * 2 + [HBM] * 9,
-        scratch=[pltpu.VMEM(a.shape, a.dtype) for a in moved] + [pltpu.SemaphoreType.DMA((9,))],
+        [SMEM] + [HBM] * 10,
+        scratch=[pltpu.SMEM(kappa.shape, kappa.dtype)]
+        + [pltpu.VMEM(a.shape, a.dtype) for a in moved]
+        + [pltpu.SemaphoreType.DMA((10,))],
         flops=4 * 10**7,
         moved=10**6,
         limit=MOST,

time: 64.2 us -> 63.4 us (0.988)
  Pallas kernels: 16.8 us -> 16 us
    pallas_call x1, Pallas kernels: 4.02 us -> 3.25 us  [column_body(): call(prepare, [shape((tiles, 2 * (OWN + tiles + 4), col_max // 2), BF16),...]
where the time goes in v4:
time: 63.4 us; the launch traced here: 63.1 us
  blocking collectives  45.8 us (72%)
  Pallas kernels  16 us (25%)
  between operations  1.31 us (2%)
    all_to_all x1, blocking collectives, column_body(): lax.all_to_all(payload, 'tile', split_axis=0, concat_axis=0, tiled=True)  20.5 us
    all_to_all x1, blocking collectives, column_body(): lax.all_to_all(back, ('tile', 'spec'), split_axis=0, concat_axis=0, tiled...  16.5 us
    pallas_call x1, Pallas kernels, column_body(): call(functools.partial(chain, tiles, layers), [shape((tiles * parts, OWN...  10.9 us
    all_to_all x1, blocking collectives, column_body(): lax.all_to_all(packed, 'spec', split_axis=0, concat_axis=0, tiled=True)  8.76 us
    pallas_call x1, Pallas kernels, column_body(): call(prepare, [shape((tiles, 2 * (OWN + tiles + 4), col_max // 2), BF16),...  3.25 us

profile of v4, /device:TPU:0, one launch (start us, length us, event | category | flops | bytes accessed | tf_op | source)
XLA Modules:
  0.0 63.1 jit_solution(8191803546533707148)
XLA Ops:
  1.3 3.3 %shard_map.122 = (bf16[8,56,512]{2,1,0:T(8,128)(2,1)}, f32[16,128]{1,0:T(8,128)}, f32[16,1024]{1,0:T(8,128)}) custom-call(s32[1]{0:T(128)S(6)} %copy.13.count_ref, f32[4]{0:T(128)} %kappa_any.1, bf16[1024,128]{1,0:T(8,128)(2,1)} %gc_any.1, bf16[4,32,32]{2,1,0:T(8,128)(2,1)} %vert_any.1, f32[4,32]{1,0:T(4,128)} %thick_any.1, f32[4,1024]{1,0:T(4,128)} %flux_any.1, ...), custom_call_target="tpu_custom_call" | custom-call | flops 40000000 | bytes 1000000 | tf_op jit(solution)/shard_map/pallas_call | solution.py:436
  4.5 0.0 copy-start.1
  4.6 20.5 %all_to_all.15.data_ref = bf16[8,56,512]{2,1,0:T(8,128)(2,1)S(1)} all-to-all(bf16[8,56,512]{2,1,0:T(8,128)(2,1)} %get-tuple-element.6), channel_id=1, replica_groups=mesh['tile'=8,'spec'=4] {'tile'}, dimensions={0} | all-to-all | bytes 917504 | tf_op jit(solution)/shard_map/all_to_all | solution.py:451
  25.1 0.0 copy-done.1
  25.1 10.9 %shard_map.123 = bf16[32,24,256]{2,1,0:T(8,128)(2,1)S(1)} custom-call(f32[16,128]{1,0:T(8,128)S(1)} %copy-done.1, bf16[8,56,512]{2,1,0:T(8,128)(2,1)S(1)} %all_to_all.15.data_ref), custom_call_target="tpu_custom_call" | custom-call | flops 10000000000 | bytes 1000000 | tf_op jit(solution)/shard_map/pallas_call | solution.py:452
  36.0 0.0 copy-start
  36.0 16.5 %all_to_all.16.data_ref = bf16[32,24,256]{2,1,0:T(8,128)(2,1)S(1)} all-to-all(bf16[32,24,256]{2,1,0:T(8,128)(2,1)S(1)} %shard_map.123), channel_id=1, replica_groups=mesh['tile'=8,'spec'=4] {'tile','spec'}, dimensions={0} | all-to-all | bytes 786432 | tf_op jit(solution)/shard_map/all_to_all | solution.py:464
  52.5 0.0 copy-done
  52.5 1.0 %shard_map.124 = bf16[4,144,256]{2,1,0:T(8,128)(2,1)S(1)} custom-call(bf16[32,24,256]{2,1,0:T(8,128)(2,1)S(1)} %all_to_all.16.data_ref, f32[16,1024]{1,0:T(8,128)S(1)} %copy-done), custom_call_target="tpu_custom_call" | custom-call | flops 1000000000 | bytes 1000000 | tf_op jit(solution)/shard_map/pallas_call | solution.py:465
  53.5 8.8 %all_to_all.17.all_ref = bf16[4,144,256]{2,1,0:T(8,128)(2,1)S(1)} all-to-all(bf16[4,144,256]{2,1,0:T(8,128)(2,1)S(1)} %shard_map.124), channel_id=1, replica_groups=mesh['tile'=8,'spec'=4] {'spec'}, dimensions={0} | all-to-all | bytes 589824 | tf_op jit(solution)/shard_map/all_to_all | solution.py:472
  62.3 0.8 %shard_map.125 = (bf16[1024,128]{1,0:T(8,128)(2,1)}, f32[4,1024]{1,0:T(4,128)}) custom-call(bf16[4,144,256]{2,1,0:T(8,128)(2,1)S(1)} %all_to_all.17.all_ref), custom_call_target="tpu_custom_call" | custom-call | flops 100000000 | bytes 1000000 | tf_op jit(solution)/shard_map/pallas_call | solution.py:474
Async XLA Ops:
  4.5 20.5 %copy-start.1 = (f32[16,128]{1,0:T(8,128)S(1)}, f32[16,128]{1,0:T(8,128)}, u32[]{:S(2)}) copy-start(f32[16,128]{1,0:T(8,128)} %get-tuple-element.5.misc_ref) | copy-start | bytes 24580
  36.0 16.5 %copy-start = (f32[16,1024]{1,0:T(8,128)S(1)}, f32[16,1024]{1,0:T(8,128)}, u32[]{:S(2)}) copy-start(f32[16,1024]{1,0:T(8,128)} %get-tuple-element.7.remap_ref) | copy-start | bytes 196612

commit v5 on v4

--- a/solution.py
+++ b/solution.py
@@ -234,7 +234,7 @@
         top = jnp.where((me * OWN) % layers == 0, jnp.concatenate(top, axis=0), mix)
         for q in range(tiles):
             piece = x_ref[last, q, :, g * WIDE : (g + 1) * WIDE]
-            back_ref[q * quarters + g] = jnp.concatenate([piece, top], axis=0).astype(BF16)
+            back_ref[g * tiles + q] = jnp.concatenate([piece, top], axis=0).astype(BF16)
 
 
 def middle(tiles, parts, layers, data_ref, remap_ref, out_ref):
@@ -245,7 +245,7 @@
     me = lax.axis_index("spec")
 
     def source(s, half):
-        return ((s % 4) * halves + half) * parts + s // 4
+        return s // 4 * tiles + (s % 4) * halves + half
 
     mix = [data_ref[source(4 * k, 1)].astype(F32)[OWN : OWN + 4, 0:species] for k in range(parts)]
     mix = jnp.concatenate(mix, axis=0)
@@ -461,7 +461,7 @@
         flops=10**10,
         moved=10**6,
     )(misc, data)[0]
-    home = lax.all_to_all(back, ("tile", "spec"), split_axis=0, concat_axis=0, tiled=True)
+    home = lax.all_to_all(back, ("spec", "tile"), split_axis=0, concat_axis=0, tiled=True)
     packed = call(
         functools.partial(middle, tiles, parts, layers),
         [shape((parts, width + OWN, WIDE), BF16)],

time: 63.4 us -> 63.8 us (level)
  no operation moved by 1% of the time
where the time goes in v5:
time: 63.8 us; the launch traced here: 63.5 us
  blocking collectives  46.1 us (72%)
  Pallas kernels  16 us (25%)
  between operations  1.31 us (2%)
    all_to_all x1, blocking collectives, column_body(): lax.all_to_all(payload, 'tile', split_axis=0, concat_axis=0, tiled=True)  20.5 us
    all_to_all x1, blocking collectives, column_body(): lax.all_to_all(back, ('spec', 'tile'), split_axis=0, concat_axis=0, tiled...  16.9 us
    pallas_call x1, Pallas kernels, column_body(): call(functools.partial(chain, tiles, layers), [shape((tiles * parts, OWN...  10.9 us
    all_to_all x1, blocking collectives, column_body(): lax.all_to_all(packed, 'spec', split_axis=0, concat_axis=0, tiled=True)  8.76 us
    pallas_call x1, Pallas kernels, column_body(): call(prepare, [shape((tiles, 2 * (OWN + tiles + 4), col_max // 2), BF16),...  3.25 us

profile of v5, /device:TPU:0, one launch (start us, length us, event | category | flops | bytes accessed | tf_op | source)
XLA Modules:
  0.0 63.5 jit_solution(2213887504611221499)
XLA Ops:
  1.3 3.3 %shard_map.122 = (bf16[8,56,512]{2,1,0:T(8,128)(2,1)}, f32[16,128]{1,0:T(8,128)}, f32[16,1024]{1,0:T(8,128)}) custom-call(s32[1]{0:T(128)S(6)} %copy.13.count_ref, f32[4]{0:T(128)} %kappa_any.1, bf16[1024,128]{1,0:T(8,128)(2,1)} %gc_any.1, bf16[4,32,32]{2,1,0:T(8,128)(2,1)} %vert_any.1, f32[4,32]{1,0:T(4,128)} %thick_any.1, f32[4,1024]{1,0:T(4,128)} %flux_any.1, ...), custom_call_target="tpu_custom_call" | custom-call | flops 40000000 | bytes 1000000 | tf_op jit(solution)/shard_map/pallas_call | solution.py:436
  4.5 0.0 copy-start.1
  4.6 20.5 %all_to_all.15.data_ref = bf16[8,56,512]{2,1,0:T(8,128)(2,1)S(1)} all-to-all(bf16[8,56,512]{2,1,0:T(8,128)(2,1)} %get-tuple-element.6), channel_id=1, replica_groups=mesh['tile'=8,'spec'=4] {'tile'}, dimensions={0} | all-to-all | bytes 917504 | tf_op jit(solution)/shard_map/all_to_all | solution.py:451
  25.1 0.0 copy-done.1
  25.1 10.9 %shard_map.123 = bf16[32,24,256]{2,1,0:T(8,128)(2,1)S(1)} custom-call(f32[16,128]{1,0:T(8,128)S(1)} %copy-done.1, bf16[8,56,512]{2,1,0:T(8,128)(2,1)S(1)} %all_to_all.15.data_ref), custom_call_target="tpu_custom_call" | custom-call | flops 10000000000 | bytes 1000000 | tf_op jit(solution)/shard_map/pallas_call | solution.py:452
  36.0 0.0 copy-start
  36.0 16.9 %all_to_all.16.data_ref = bf16[32,24,256]{2,1,0:T(8,128)(2,1)S(1)} all-to-all(bf16[32,24,256]{2,1,0:T(8,128)(2,1)S(1)} %shard_map.123), channel_id=1, replica_groups=mesh['tile'=8,'spec'=4] {'spec','tile'}, dimensions={0} | all-to-all | bytes 786432 | tf_op jit(solution)/shard_map/all_to_all | solution.py:464
  52.9 0.0 copy-done
  52.9 1.0 %shard_map.124 = bf16[4,144,256]{2,1,0:T(8,128)(2,1)S(1)} custom-call(bf16[32,24,256]{2,1,0:T(8,128)(2,1)S(1)} %all_to_all.16.data_ref, f32[16,1024]{1,0:T(8,128)S(1)} %copy-done), custom_call_target="tpu_custom_call" | custom-call | flops 1000000000 | bytes 1000000 | tf_op jit(solution)/shard_map/pallas_call | solution.py:465
  53.9 8.8 %all_to_all.17.all_ref = bf16[4,144,256]{2,1,0:T(8,128)(2,1)S(1)} all-to-all(bf16[4,144,256]{2,1,0:T(8,128)(2,1)S(1)} %shard_map.124), channel_id=1, replica_groups=mesh['tile'=8,'spec'=4] {'spec'}, dimensions={0} | all-to-all | bytes 589824 | tf_op jit(solution)/shard_map/all_to_all | solution.py:472
  62.6 0.8 %shard_map.125 = (bf16[1024,128]{1,0:T(8,128)(2,1)}, f32[4,1024]{1,0:T(4,128)}) custom-call(bf16[4,144,256]{2,1,0:T(8,128)(2,1)S(1)} %all_to_all.17.all_ref), custom_call_target="tpu_custom_call" | custom-call | flops 100000000 | bytes 1000000 | tf_op jit(solution)/shard_map/pallas_call | solution.py:474
Async XLA Ops:
  4.5 20.5 %copy-start.1 = (f32[16,128]{1,0:T(8,128)S(1)}, f32[16,128]{1,0:T(8,128)}, u32[]{:S(2)}) copy-start(f32[16,128]{1,0:T(8,128)} %get-tuple-element.5.misc_ref) | copy-start | bytes 24580
  36.0 16.9 %copy-start = (f32[16,1024]{1,0:T(8,128)S(1)}, f32[16,1024]{1,0:T(8,128)}, u32[]{:S(2)}) copy-start(f32[16,1024]{1,0:T(8,128)} %get-tuple-element.7.remap_ref) | copy-start | bytes 196612

commit v6 on v4

--- a/solution.py
+++ b/solution.py
@@ -21,12 +21,12 @@
 MOST = 60 * 1024 * 1024
 
 
-def call(kernel, outs, specs, scratch=(), flops=0, moved=0, limit=LIMIT):
+def call(kernel, outs, specs, scratch=(), flops=0, moved=0, limit=LIMIT, first=VMEM):
     return pl.pallas_call(
         kernel,
         out_shape=outs,
         in_specs=specs,
-        out_specs=[VMEM] * len(outs),
+        out_specs=[first] + [VMEM] * (len(outs) - 1),
         scratch_shapes=scratch,
         compiler_params=pltpu.CompilerParams(vmem_limit_bytes=limit),
         cost_estimate=pl.CostEstimate(flops=flops, bytes_accessed=moved, transcendentals=0),
@@ -125,7 +125,9 @@
     vt = jnp.where(rows == cols, v, 0.0).T.astype(BF16)
     hi = lax.Precision.HIGHEST
     v2 = nn(vt, vt)
-    v4 = nn(v2, v2, hi)
+    large = v2.astype(BF16)
+    small = (v2 - large.astype(F32)).astype(BF16)
+    v4 = nn(large, large) + (nn(large, small) + nn(small, large))
     th = jnp.concatenate([thick_ref[s : s + 1, :] for s in range(species)], axis=1)
     misc_ref[0:8] = nt(jnp.broadcast_to(th, (8, width)), v4, hi)
     rates = [jnp.full((1, width), kappa_ref[s], F32) for s in range(species)]
@@ -286,16 +288,21 @@
         out_ref[k] = jnp.concatenate(rows, axis=0).astype(BF16)
 
 
-def settle(all_ref, state_ref, bottom_ref):
+def settle(all_ref, state_any, bottom_ref, state_ref, sems):
     parts, rows, wide = all_ref.shape
     width = state_ref.shape[1]
     total = jnp.zeros((rows - width, wide), F32)
+    copies = []
     for k in range(parts):
-        state = all_ref[k, 0:width].astype(F32)
-        state_ref[k * wide : (k + 1) * wide, :] = state.T.astype(BF16)
+        here = pl.ds(k * wide, wide)
+        state_ref[here, :] = all_ref[k, 0:width].astype(F32).T.astype(BF16)
+        copies.append(pltpu.make_async_copy(state_ref.at[here], state_any.at[here], sems.at[k]))
+        copies[-1].start()
         total = total + all_ref[k, width:].astype(F32)
     pieces = [total[h * 4 : h * 4 + 4] for h in range(parts)]
     bottom_ref[...] = jnp.concatenate(pieces, axis=1)
+    for copy in copies:
+        copy.wait()
 
 
 def shifted(block, axis, distance):
@@ -471,7 +478,8 @@
     )(home, remap)[0]
     every = lax.all_to_all(packed, "spec", split_axis=0, concat_axis=0, tiled=True)
     outs = [shape((col_max, width), BF16), shape((4, col_max), F32)]
-    return tuple(call(settle, outs, [VMEM], flops=10**8, moved=10**6)(every))
+    scratch = [pltpu.VMEM((col_max, width), BF16), pltpu.SemaphoreType.DMA((parts,))]
+    return tuple(call(settle, outs, [VMEM], scratch, 10**8, 10**6, first=HBM)(every))
 
 
 def body(*args):

time: 63.4 us -> 64 us (level)
  no operation moved by 1% of the time
where the time goes in v6:
time: 64 us; the launch traced here: 63.6 us
  blocking collectives  45.8 us (72%)
  Pallas kernels  16.5 us (26%)
  between operations  1.31 us (2%)
    all_to_all x1, blocking collectives, column_body(): lax.all_to_all(payload, 'tile', split_axis=0, concat_axis=0, tiled=True)  20.5 us
    all_to_all x1, blocking collectives, column_body(): lax.all_to_all(back, ('tile', 'spec'), split_axis=0, concat_axis=0, tiled...  16.5 us
    pallas_call x1, Pallas kernels, column_body(): call(functools.partial(chain, tiles, layers), [shape((tiles * parts, OWN...  10.9 us
    all_to_all x1, blocking collectives, column_body(): lax.all_to_all(packed, 'spec', split_axis=0, concat_axis=0, tiled=True)  8.76 us
    pallas_call x1, Pallas kernels, column_body(): call(prepare, [shape((tiles, 2 * (OWN + tiles + 4), col_max // 2), BF16),...  3.2 us
    pallas_call x1, Pallas kernels, column_body(): call(settle, outs, [VMEM], scratch, 10 ** 8, 10 ** 6, first=HBM)(every)  1.43 us

profile of v6, /device:TPU:0, one launch (start us, length us, event | category | flops | bytes accessed | tf_op | source)
XLA Modules:
  0.0 63.6 jit_solution(4085955807577405838)
XLA Ops:
  1.3 3.2 %shard_map.122 = (bf16[8,56,512]{2,1,0:T(8,128)(2,1)}, f32[16,128]{1,0:T(8,128)}, f32[16,1024]{1,0:T(8,128)}) custom-call(s32[1]{0:T(128)S(6)} %copy.13.count_ref, f32[4]{0:T(128)} %kappa_any.1, bf16[1024,128]{1,0:T(8,128)(2,1)} %gc_any.1, bf16[4,32,32]{2,1,0:T(8,128)(2,1)} %vert_any.1, f32[4,32]{1,0:T(4,128)} %thick_any.1, f32[4,1024]{1,0:T(4,128)} %flux_any.1, ...), custom_call_target="tpu_custom_call" | custom-call | flops 40000000 | bytes 1000000 | tf_op jit(solution)/shard_map/pallas_call | solution.py:443
  4.5 0.0 copy-start.1
  4.5 20.5 %all_to_all.15.data_ref = bf16[8,56,512]{2,1,0:T(8,128)(2,1)S(1)} all-to-all(bf16[8,56,512]{2,1,0:T(8,128)(2,1)} %get-tuple-element.6), channel_id=1, replica_groups=mesh['tile'=8,'spec'=4] {'tile'}, dimensions={0} | all-to-all | bytes 917504 | tf_op jit(solution)/shard_map/all_to_all | solution.py:458
  25.0 0.0 copy-done.1
  25.0 10.9 %shard_map.123 = bf16[32,24,256]{2,1,0:T(8,128)(2,1)S(1)} custom-call(f32[16,128]{1,0:T(8,128)S(1)} %copy-done.1, bf16[8,56,512]{2,1,0:T(8,128)(2,1)S(1)} %all_to_all.15.data_ref), custom_call_target="tpu_custom_call" | custom-call | flops 10000000000 | bytes 1000000 | tf_op jit(solution)/shard_map/pallas_call | solution.py:459
  36.0 0.0 copy-start
  36.0 16.5 %all_to_all.16.data_ref = bf16[32,24,256]{2,1,0:T(8,128)(2,1)S(1)} all-to-all(bf16[32,24,256]{2,1,0:T(8,128)(2,1)S(1)} %shard_map.123), channel_id=1, replica_groups=mesh['tile'=8,'spec'=4] {'tile','spec'}, dimensions={0} | all-to-all | bytes 786432 | tf_op jit(solution)/shard_map/all_to_all | solution.py:471
  52.4 0.0 copy-done
  52.5 1.0 %shard_map.124 = bf16[4,144,256]{2,1,0:T(8,128)(2,1)S(1)} custom-call(bf16[32,24,256]{2,1,0:T(8,128)(2,1)S(1)} %all_to_all.16.data_ref, f32[16,1024]{1,0:T(8,128)S(1)} %copy-done), custom_call_target="tpu_custom_call" | custom-call | flops 1000000000 | bytes 1000000 | tf_op jit(solution)/shard_map/pallas_call | solution.py:472
  53.4 8.8 %all_to_all.17.all_ref = bf16[4,144,256]{2,1,0:T(8,128)(2,1)S(1)} all-to-all(bf16[4,144,256]{2,1,0:T(8,128)(2,1)S(1)} %shard_map.124), channel_id=1, replica_groups=mesh['tile'=8,'spec'=4] {'spec'}, dimensions={0} | all-to-all | bytes 589824 | tf_op jit(solution)/shard_map/all_to_all | solution.py:479
  62.2 1.4 %shard_map.125 = (bf16[1024,128]{1,0:T(8,128)(2,1)}, f32[4,1024]{1,0:T(4,128)}) custom-call(bf16[4,144,256]{2,1,0:T(8,128)(2,1)S(1)} %all_to_all.17.all_ref), custom_call_target="tpu_custom_call" | custom-call | flops 100000000 | bytes 1000000 | tf_op jit(solution)/shard_map/pallas_call | solution.py:482
Async XLA Ops:
  4.5 20.5 %copy-start.1 = (f32[16,128]{1,0:T(8,128)S(1)}, f32[16,128]{1,0:T(8,128)}, u32[]{:S(2)}) copy-start(f32[16,128]{1,0:T(8,128)} %get-tuple-element.5.misc_ref) | copy-start | bytes 24580
  36.0 16.5 %copy-start = (f32[16,1024]{1,0:T(8,128)S(1)}, f32[16,1024]{1,0:T(8,128)}, u32[]{:S(2)}) copy-start(f32[16,1024]{1,0:T(8,128)} %get-tuple-element.7.remap_ref) | copy-start | bytes 196612

commit v7 on v4

--- a/solution.py
+++ b/solution.py
@@ -291,8 +291,7 @@
     width = state_ref.shape[1]
     total = jnp.zeros((rows - width, wide), F32)
     for k in range(parts):
-        state = all_ref[k, 0:width].astype(F32)
-        state_ref[k * wide : (k + 1) * wide, :] = state.T.astype(BF16)
+        state_ref[k * wide : (k + 1) * wide, :] = all_ref[k, 0:width].T
         total = total + all_ref[k, width:].astype(F32)
     pieces = [total[h * 4 : h * 4 + 4] for h in range(parts)]
     bottom_ref[...] = jnp.concatenate(pieces, axis=1)

time: 63.4 us -> 63.4 us (level)
  no operation moved by 1% of the time
where the time goes in v7:
time: 63.4 us; the launch traced here: 63.1 us
  blocking collectives  45.8 us (72%)
  Pallas kernels  16 us (25%)
  between operations  1.31 us (2%)
    all_to_all x1, blocking collectives, column_body(): lax.all_to_all(payload, 'tile', split_axis=0, concat_axis=0, tiled=True)  20.5 us
    all_to_all x1, blocking collectives, column_body(): lax.all_to_all(back, ('tile', 'spec'), split_axis=0, concat_axis=0, tiled...  16.5 us
    pallas_call x1, Pallas kernels, column_body(): call(functools.partial(chain, tiles, layers), [shape((tiles * parts, OWN...  10.9 us
    all_to_all x1, blocking collectives, column_body(): lax.all_to_all(packed, 'spec', split_axis=0, concat_axis=0, tiled=True)  8.76 us
    pallas_call x1, Pallas kernels, column_body(): call(prepare, [shape((tiles, 2 * (OWN + tiles + 4), col_max // 2), BF16),...  3.25 us

profile of v7, /device:TPU:0, one launch (start us, length us, event | category | flops | bytes accessed | tf_op | source)
XLA Modules:
  0.0 63.1 jit_solution(8633440073009224151)
XLA Ops:
  1.3 3.3 %shard_map.122 = (bf16[8,56,512]{2,1,0:T(8,128)(2,1)}, f32[16,128]{1,0:T(8,128)}, f32[16,1024]{1,0:T(8,128)}) custom-call(s32[1]{0:T(128)S(6)} %copy.13.count_ref, f32[4]{0:T(128)} %kappa_any.1, bf16[1024,128]{1,0:T(8,128)(2,1)} %gc_any.1, bf16[4,32,32]{2,1,0:T(8,128)(2,1)} %vert_any.1, f32[4,32]{1,0:T(4,128)} %thick_any.1, f32[4,1024]{1,0:T(4,128)} %flux_any.1, ...), custom_call_target="tpu_custom_call" | custom-call | flops 40000000 | bytes 1000000 | tf_op jit(solution)/shard_map/pallas_call | solution.py:435
  4.5 0.0 copy-start.1
  4.6 20.5 %all_to_all.15.data_ref = bf16[8,56,512]{2,1,0:T(8,128)(2,1)S(1)} all-to-all(bf16[8,56,512]{2,1,0:T(8,128)(2,1)} %get-tuple-element.6), channel_id=1, replica_groups=mesh['tile'=8,'spec'=4] {'tile'}, dimensions={0} | all-to-all | bytes 917504 | tf_op jit(solution)/shard_map/all_to_all | solution.py:450
  25.1 0.0 copy-done.1
  25.1 10.9 %shard_map.123 = bf16[32,24,256]{2,1,0:T(8,128)(2,1)S(1)} custom-call(f32[16,128]{1,0:T(8,128)S(1)} %copy-done.1, bf16[8,56,512]{2,1,0:T(8,128)(2,1)S(1)} %all_to_all.15.data_ref), custom_call_target="tpu_custom_call" | custom-call | flops 10000000000 | bytes 1000000 | tf_op jit(solution)/shard_map/pallas_call | solution.py:451
  36.0 0.0 copy-start
  36.0 16.5 %all_to_all.16.data_ref = bf16[32,24,256]{2,1,0:T(8,128)(2,1)S(1)} all-to-all(bf16[32,24,256]{2,1,0:T(8,128)(2,1)S(1)} %shard_map.123), channel_id=1, replica_groups=mesh['tile'=8,'spec'=4] {'tile','spec'}, dimensions={0} | all-to-all | bytes 786432 | tf_op jit(solution)/shard_map/all_to_all | solution.py:463
  52.5 0.0 copy-done
  52.5 1.0 %shard_map.124 = bf16[4,144,256]{2,1,0:T(8,128)(2,1)S(1)} custom-call(bf16[32,24,256]{2,1,0:T(8,128)(2,1)S(1)} %all_to_all.16.data_ref, f32[16,1024]{1,0:T(8,128)S(1)} %copy-done), custom_call_target="tpu_custom_call" | custom-call | flops 1000000000 | bytes 1000000 | tf_op jit(solution)/shard_map/pallas_call | solution.py:464
  53.5 8.8 %all_to_all.17.all_ref = bf16[4,144,256]{2,1,0:T(8,128)(2,1)S(1)} all-to-all(bf16[4,144,256]{2,1,0:T(8,128)(2,1)S(1)} %shard_map.124), channel_id=1, replica_groups=mesh['tile'=8,'spec'=4] {'spec'}, dimensions={0} | all-to-all | bytes 589824 | tf_op jit(solution)/shard_map/all_to_all | solution.py:471
  62.3 0.8 %shard_map.125 = (bf16[1024,128]{1,0:T(8,128)(2,1)}, f32[4,1024]{1,0:T(4,128)}) custom-call(bf16[4,144,256]{2,1,0:T(8,128)(2,1)S(1)} %all_to_all.17.all_ref), custom_call_target="tpu_custom_call" | custom-call | flops 100000000 | bytes 1000000 | tf_op jit(solution)/shard_map/pallas_call | solution.py:473
Async XLA Ops:
  4.5 20.5 %copy-start.1 = (f32[16,128]{1,0:T(8,128)S(1)}, f32[16,128]{1,0:T(8,128)}, u32[]{:S(2)}) copy-start(f32[16,128]{1,0:T(8,128)} %get-tuple-element.5.misc_ref) | copy-start | bytes 24580
  36.0 16.5 %copy-start = (f32[16,1024]{1,0:T(8,128)S(1)}, f32[16,1024]{1,0:T(8,128)}, u32[]{:S(2)}) copy-start(f32[16,1024]{1,0:T(8,128)} %get-tuple-element.7.remap_ref) | copy-start | bytes 196612
